TPU v7x, 512 devices: a whole 4x8x8 slice. The times are simulated.
512 devices in a mesh: frames: 128 (over z, y, x_lo), heads: 4 (over x_hi, core).
Axes of the slice: x: 4 (x_hi: 2, x_lo: 2; x = x_hi * 2 + x_lo), y: 8, z: 8, core: 2. Of those that a mesh axis runs over, the one named last changes fastest.
Arguments:
- queries: bfloat16 [12288, 2560], P('frames', 'heads'), may hold values from -40 to 40
- keys_values: bfloat16 [2, 12288, 2560], P(None, 'frames', 'heads'), may hold values from -40 to 40
- out_weight: bfloat16 [2560, 5120], P('heads', 'frames'), may hold values from -0.5 to 0.5
Outputs:
- projected: bfloat16 [12288, 5120], P('frames', 'heads')
All inputs are finite; a program needn't handle non-finite values.
Results may differ from a plain program's by a relative error of at most 0.015.
Values may be sent and summed in bfloat16 or wider, within the bound.
A program may use at most 64 MiB of HBM per device.

v0:
```python
import jax
import jax.numpy as jnp
from jax import lax
from jax.sharding import PartitionSpec as P

HD = 128
TPF = 32
FR_DEV = 3
reach_cap = 32


def from_behind(x, axis, by):
    devices = lax.axis_size(axis)
    return lax.ppermute(x, axis, [(i, (i + by) % devices) for i in range(devices)])


def on_device(queries, keys_values, out_weight):
    total_frames = lax.axis_size("frames") * FR_DEV
    reach = min(reach_cap, (total_frames - 1) // 2)
    steps = (reach + FR_DEV - 1) // FR_DEV
    width = keys_values.shape[2]
    span = FR_DEV + 2 * reach
    stacked = keys_values.reshape(2, FR_DEV, TPF, width)
    pieces = []
    for offset in range(-steps, steps + 1):
        if offset == 0:
            pieces.append(stacked)
        else:
            pieces.append(from_behind(stacked, "frames", -offset))
    window = jnp.concatenate(pieces, axis=1)
    lower_frame = steps * FR_DEV - reach
    extended = window[:, lower_frame : lower_frame + span]
    keys_ext = extended[0].reshape(span * TPF, width)
    values_ext = extended[1].reshape(span * TPF, width)
    row_frame = jnp.arange(FR_DEV * TPF, dtype=jnp.int32) // TPF
    col_frame = jnp.arange(span * TPF, dtype=jnp.int32) // TPF
    allowed = (col_frame[None, :] >= row_frame[:, None]) & (
        col_frame[None, :] <= row_frame[:, None] + 2 * reach
    )
    results = []
    for head in range(width // HD):
        lower = head * HD
        query_cols = queries[:, lower : lower + HD]
        key_cols = keys_ext[:, lower : lower + HD]
        scores = lax.dot_general(
            query_cols, key_cols, (((1,), (1,)), ((), ())), preferred_element_type=jnp.float32
        )
        scores = scores * HD ** (-0.5)
        top = jnp.max(jnp.where(allowed, scores, -1e30), axis=1, keepdims=True)
        weights = jnp.where(allowed, jnp.exp(scores - top), 0.0)
        probs = (weights / jnp.sum(weights, axis=1, keepdims=True)).astype(jnp.bfloat16)
        results.append(
            jnp.dot(
                probs, values_ext[:, lower : lower + HD], preferred_element_type=jnp.float32
            ).astype(jnp.bfloat16)
        )
    attended = jnp.concatenate(results, axis=1)
    partial_rows = jnp.dot(
        attended,
        lax.all_gather(out_weight, "frames", axis=1, tiled=True),
        preferred_element_type=jnp.float32,
    )
    return lax.psum_scatter(
        partial_rows.astype(jnp.bfloat16), "heads", scatter_dimension=1, tiled=True
    )


def solution(mesh):
    in_specs = (P("frames", "heads"), P(None, "frames", "heads"), P("heads", "frames"))
    out_specs = P("frames", "heads")
    return jax.shard_map(
        on_device, mesh=mesh, in_specs=in_specs, out_specs=out_specs, check_vma=False
    )
```

profile of v0, /device:TPU:1, one launch (start us, length us, event | category | flops | bytes accessed | tf_op | source)
XLA Modules:
  0.0 740.1 jit_solution(7605853426506819960)
XLA Ops:
  7.3 8.4 %collective-permute-start = (bf16[2,3,32,640]{3,2,1,0:T(8,128)(2,1)}, bf16[2,3,32,640]{3,2,1,0:T(8,128)(2,1)S(1)}, u32[]{:S(2)}, u32[]{:S(2)}) collective-permute-start(bf16[2,3,32,640]{3,2,1,0:T(8,128)(2,1)} %bitcast.25), channel_id=1, source_target_pairs={{0,44},{4,48},{8,52},{12,56},{16,60},{20,64},{24,68},{28,72},{32,7... | collective-permute-start | bytes 737288 | tf_op jit(solution)/shard_map/ppermute | solution.py:14
  15.7 4.6 collective-permute-start.1
  20.3 4.8 collective-permute-start.2
  25.2 6.2 collective-permute-start.3
  31.4 4.4 collective-permute-start.4
  40.2 8.4 %collective-permute-done.1 = bf16[2,3,32,640]{3,2,1,0:T(8,128)(2,1)S(1)} collective-permute-done((bf16[2,3,32,640]{3,2,1,0:T(8,128)(2,1)}, bf16[2,3,32,640]{3,2,1,0:T(8,128)(2,1)S(1)}, u32[]{:S(2)}, u32[]{:S(2)}) %collective-permute-start.1) | collective-permute-done | bytes 245792 | tf_op jit(solution)/shard_map/ppermute | solution.py:14
  48.6 6.4 collective-permute-start.6
  55.0 6.1 collective-permute-done.2
  61.1 19.7 %collective-permute-start.7 = (bf16[2,3,32,640]{3,2,1,0:T(8,128)(2,1)}, bf16[2,3,32,640]{3,2,1,0:T(8,128)(2,1)S(1)}, u32[]{:S(2)}, u32[]{:S(2)}) collective-permute-start(bf16[2,3,32,640]{3,2,1,0:T(8,128)(2,1)} %bitcast.32), channel_id=1, source_target_pairs={{0,16},{4,20},{8,24},{12,28},{16,32},{20,36},{24,40},{28,44},{32,4... | collective-permute-start | bytes 737288 | tf_op jit(solution)/shard_map/ppermute | solution.py:14
  80.8 6.9 collective-permute-start.8
  87.8 6.6 collective-permute-start.9
  96.4 7.6 %collective-permute-start.11 = (bf16[2,3,32,640]{3,2,1,0:T(8,128)(2,1)}, bf16[2,3,32,640]{3,2,1,0:T(8,128)(2,1)S(1)}, u32[]{:S(2)}, u32[]{:S(2)}) collective-permute-start(bf16[2,3,32,640]{3,2,1,0:T(8,128)(2,1)} %bitcast.36), channel_id=1, source_target_pairs={{0,508},{4,0},{8,4},{12,8},{16,12},{20,16},{24,20},{28,24},{32,28}... | collective-permute-start | bytes 737288 | tf_op jit(solution)/shard_map/ppermute | solution.py:14
  106.6 7.4 %collective-permute-start.12 = (bf16[2,3,32,640]{3,2,1,0:T(8,128)(2,1)}, bf16[2,3,32,640]{3,2,1,0:T(8,128)(2,1)S(1)}, u32[]{:S(2)}, u32[]{:S(2)}) collective-permute-start(bf16[2,3,32,640]{3,2,1,0:T(8,128)(2,1)} %bitcast.37), channel_id=1, source_target_pairs={{0,504},{4,508},{8,0},{12,4},{16,8},{20,12},{24,16},{28,20},{32,24... | collective-permute-start | bytes 737288 | tf_op jit(solution)/shard_map/ppermute | solution.py:14
  120.4 5.2 collective-permute-start.14
  125.7 6.7 collective-permute-done.10
  135.3 7.5 %collective-permute-start.16 = (bf16[2,3,32,640]{3,2,1,0:T(8,128)(2,1)S(1)}, bf16[2,3,32,640]{3,2,1,0:T(8,128)(2,1)S(1)}, u32[]{:S(2)}, u32[]{:S(2)}) collective-permute-start(bf16[2,3,32,640]{3,2,1,0:T(8,128)(2,1)S(1)} %bitcast.42), channel_id=1, source_target_pairs={{0,488},{4,492},{8,496},{12,500},{16,504},{20,508},{24,0},{28,4},{... | collective-permute-start | bytes 737288 | tf_op jit(solution)/shard_map/ppermute | solution.py:14
  142.9 7.3 collective-permute-start.17
  155.2 8.1 %collective-permute-start.20 = (bf16[2,3,32,640]{3,2,1,0:T(8,128)(2,1)S(1)}, bf16[2,3,32,640]{3,2,1,0:T(8,128)(2,1)S(1)}, u32[]{:S(2)}, u32[]{:S(2)}) collective-permute-start(bf16[2,3,32,640]{3,2,1,0:T(8,128)(2,1)S(1)} %bitcast.46), channel_id=1, source_target_pairs={{0,472},{4,476},{8,480},{12,484},{16,488},{20,492},{24,496},{28,50... | collective-permute-start | bytes 737288 | tf_op jit(solution)/shard_map/ppermute | solution.py:14
  163.3 9.2 %collective-permute-done.16 = bf16[2,3,32,640]{3,2,1,0:T(8,128)(2,1)S(1)} collective-permute-done((bf16[2,3,32,640]{3,2,1,0:T(8,128)(2,1)S(1)}, bf16[2,3,32,640]{3,2,1,0:T(8,128)(2,1)S(1)}, u32[]{:S(2)}, u32[]{:S(2)}) %collective-permute-start.16) | collective-permute-done | bytes 245792 | tf_op jit(solution)/shard_map/ppermute | solution.py:14
  174.5 6.0 collective-permute-done.17
  180.6 32.5 %collective-permute-done.20 = bf16[2,3,32,640]{3,2,1,0:T(8,128)(2,1)S(1)} collective-permute-done((bf16[2,3,32,640]{3,2,1,0:T(8,128)(2,1)S(1)}, bf16[2,3,32,640]{3,2,1,0:T(8,128)(2,1)S(1)}, u32[]{:S(2)}, u32[]{:S(2)}) %collective-permute-start.20) | collective-permute-done | bytes 245792 | tf_op jit(solution)/shard_map/ppermute | solution.py:14
  219.5 395.4 %all-gather.2.cloned.1.call-done = bf16[640,5120]{0,1:T(8,128)(2,1)} async-done(((bf16[640,40]{0,1:T(8,128)(2,1)}), bf16[640,5120]{0,1:T(8,128)(2,1)}) %all-gather.2.cloned.1.call-update) | async-done | bytes 6553616 | tf_op jit(solution)/shard_map/all_gather | solution.py:60
  614.9 5.9 convolution_convert_fusion
  620.9 112.4 %reduce-scatter.2.cloned.1.call-done = bf16[96,1280]{1,0:T(8,128)(2,1)} async-done(((bf16[96,5120]{1,0:T(8,128)(2,1)}), bf16[96,1280]{1,0:T(8,128)(2,1)}) %reduce-scatter.2.cloned.1.call-update) | async-done | bytes 245776 | tf_op jit(solution)/shard_map/reduce_scatter | solution.py:63
  (68 shorter events, 32.4 us)
Async XLA Ops:
  6.5 608.4 %all-gather.2.cloned.1.call-start = ((), (), s32[]{:S(2)}) async-start(), calls=%async_computation.1 | async-start | bytes 6604800 | tf_op jit(solution)/shard_map/all_gather | solution.py:60
  7.3 726.0 %reduce-scatter.2.cloned.1.call-start = ((), (), s32[]{:S(2)}) async-start(), calls=%async_computation.2 | async-start | bytes 1228800 | tf_op jit(solution)/shard_map/reduce_scatter | solution.py:63
  7.3 28.5 %collective-permute-start = (bf16[2,3,32,640]{3,2,1,0:T(8,128)(2,1)}, bf16[2,3,32,640]{3,2,1,0:T(8,128)(2,1)S(1)}, u32[]{:S(2)}, u32[]{:S(2)}) collective-permute-start(bf16[2,3,32,640]{3,2,1,0:T(8,128)(2,1)} %bitcast.25), channel_id=1, source_target_pairs={{0,44},{4,48},{8,52},{12,56},{16,60},{20,64},{24,68},{28,72},{32,7... | collective-permute-start | bytes 737288 | tf_op jit(solution)/shard_map/ppermute | solution.py:14
  15.7 32.9 %collective-permute-start.1 = (bf16[2,3,32,640]{3,2,1,0:T(8,128)(2,1)}, bf16[2,3,32,640]{3,2,1,0:T(8,128)(2,1)S(1)}, u32[]{:S(2)}, u32[]{:S(2)}) collective-permute-start(bf16[2,3,32,640]{3,2,1,0:T(8,128)(2,1)} %bitcast.26), channel_id=1, source_target_pairs={{0,40},{4,44},{8,48},{12,52},{16,56},{20,60},{24,64},{28,68},{32,7... | collective-permute-start | bytes 737288 | tf_op jit(solution)/shard_map/ppermute | solution.py:14
  20.3 40.8 %collective-permute-start.2 = (bf16[2,3,32,640]{3,2,1,0:T(8,128)(2,1)}, bf16[2,3,32,640]{3,2,1,0:T(8,128)(2,1)S(1)}, u32[]{:S(2)}, u32[]{:S(2)}) collective-permute-start(bf16[2,3,32,640]{3,2,1,0:T(8,128)(2,1)} %bitcast.27), channel_id=1, source_target_pairs={{0,36},{4,40},{8,44},{12,48},{16,52},{20,56},{24,60},{28,64},{32,6... | collective-permute-start | bytes 737288 | tf_op jit(solution)/shard_map/ppermute | solution.py:14
  25.2 55.7 %collective-permute-start.3 = (bf16[2,3,32,640]{3,2,1,0:T(8,128)(2,1)}, bf16[2,3,32,640]{3,2,1,0:T(8,128)(2,1)S(1)}, u32[]{:S(2)}, u32[]{:S(2)}) collective-permute-start(bf16[2,3,32,640]{3,2,1,0:T(8,128)(2,1)} %bitcast.28), channel_id=1, source_target_pairs={{0,32},{4,36},{8,40},{12,44},{16,48},{20,52},{24,56},{28,60},{32,6... | collective-permute-start | bytes 737288 | tf_op jit(solution)/shard_map/ppermute | solution.py:14
  31.4 56.4 %collective-permute-start.4 = (bf16[2,3,32,640]{3,2,1,0:T(8,128)(2,1)}, bf16[2,3,32,640]{3,2,1,0:T(8,128)(2,1)S(1)}, u32[]{:S(2)}, u32[]{:S(2)}) collective-permute-start(bf16[2,3,32,640]{3,2,1,0:T(8,128)(2,1)} %bitcast.29), channel_id=1, source_target_pairs={{0,28},{4,32},{8,36},{12,40},{16,44},{20,48},{24,52},{28,56},{32,6... | collective-permute-start | bytes 737288 | tf_op jit(solution)/shard_map/ppermute | solution.py:14
  35.8 58.6 %collective-permute-start.5 = (bf16[2,3,32,640]{3,2,1,0:T(8,128)(2,1)}, bf16[2,3,32,640]{3,2,1,0:T(8,128)(2,1)S(1)}, u32[]{:S(2)}, u32[]{:S(2)}) collective-permute-start(bf16[2,3,32,640]{3,2,1,0:T(8,128)(2,1)} %bitcast.30), channel_id=1, source_target_pairs={{0,24},{4,28},{8,32},{12,36},{16,40},{20,44},{24,48},{28,52},{32,5... | collective-permute-start | bytes 737288 | tf_op jit(solution)/shard_map/ppermute | solution.py:14
  48.6 47.8 %collective-permute-start.6 = (bf16[2,3,32,640]{3,2,1,0:T(8,128)(2,1)}, bf16[2,3,32,640]{3,2,1,0:T(8,128)(2,1)S(1)}, u32[]{:S(2)}, u32[]{:S(2)}) collective-permute-start(bf16[2,3,32,640]{3,2,1,0:T(8,128)(2,1)} %bitcast.31), channel_id=1, source_target_pairs={{0,20},{4,24},{8,28},{12,32},{16,36},{20,40},{24,44},{28,48},{32,5... | collective-permute-start | bytes 737288 | tf_op jit(solution)/shard_map/ppermute | solution.py:14
  61.1 45.5 %collective-permute-start.7 = (bf16[2,3,32,640]{3,2,1,0:T(8,128)(2,1)}, bf16[2,3,32,640]{3,2,1,0:T(8,128)(2,1)S(1)}, u32[]{:S(2)}, u32[]{:S(2)}) collective-permute-start(bf16[2,3,32,640]{3,2,1,0:T(8,128)(2,1)} %bitcast.32), channel_id=1, source_target_pairs={{0,16},{4,20},{8,24},{12,28},{16,32},{20,36},{24,40},{28,44},{32,4... | collective-permute-start | bytes 737288 | tf_op jit(solution)/shard_map/ppermute | solution.py:14
  80.8 35.7 %collective-permute-start.8 = (bf16[2,3,32,640]{3,2,1,0:T(8,128)(2,1)}, bf16[2,3,32,640]{3,2,1,0:T(8,128)(2,1)S(1)}, u32[]{:S(2)}, u32[]{:S(2)}) collective-permute-start(bf16[2,3,32,640]{3,2,1,0:T(8,128)(2,1)} %bitcast.33), channel_id=1, source_target_pairs={{0,12},{4,16},{8,20},{12,24},{16,28},{20,32},{24,36},{28,40},{32,4... | collective-permute-start | bytes 737288 | tf_op jit(solution)/shard_map/ppermute | solution.py:14
  87.8 32.6 %collective-permute-start.9 = (bf16[2,3,32,640]{3,2,1,0:T(8,128)(2,1)}, bf16[2,3,32,640]{3,2,1,0:T(8,128)(2,1)S(1)}, u32[]{:S(2)}, u32[]{:S(2)}) collective-permute-start(bf16[2,3,32,640]{3,2,1,0:T(8,128)(2,1)} %bitcast.34), channel_id=1, source_target_pairs={{0,8},{4,12},{8,16},{12,20},{16,24},{20,28},{24,32},{28,36},{32,40... | collective-permute-start | bytes 737288 | tf_op jit(solution)/shard_map/ppermute | solution.py:14
  94.4 37.9 %collective-permute-start.10 = (bf16[2,3,32,640]{3,2,1,0:T(8,128)(2,1)}, bf16[2,3,32,640]{3,2,1,0:T(8,128)(2,1)S(1)}, u32[]{:S(2)}, u32[]{:S(2)}) collective-permute-start(bf16[2,3,32,640]{3,2,1,0:T(8,128)(2,1)} %bitcast.35), channel_id=1, source_target_pairs={{0,4},{4,8},{8,12},{12,16},{16,20},{20,24},{24,28},{28,32},{32,36}... | collective-permute-start | bytes 737288 | tf_op jit(solution)/shard_map/ppermute | solution.py:14
  96.4 38.9 %collective-permute-start.11 = (bf16[2,3,32,640]{3,2,1,0:T(8,128)(2,1)}, bf16[2,3,32,640]{3,2,1,0:T(8,128)(2,1)S(1)}, u32[]{:S(2)}, u32[]{:S(2)}) collective-permute-start(bf16[2,3,32,640]{3,2,1,0:T(8,128)(2,1)} %bitcast.36), channel_id=1, source_target_pairs={{0,508},{4,0},{8,4},{12,8},{16,12},{20,16},{24,20},{28,24},{32,28}... | collective-permute-start | bytes 737288 | tf_op jit(solution)/shard_map/ppermute | solution.py:14
  106.6 36.3 %collective-permute-start.12 = (bf16[2,3,32,640]{3,2,1,0:T(8,128)(2,1)}, bf16[2,3,32,640]{3,2,1,0:T(8,128)(2,1)S(1)}, u32[]{:S(2)}, u32[]{:S(2)}) collective-permute-start(bf16[2,3,32,640]{3,2,1,0:T(8,128)(2,1)} %bitcast.37), channel_id=1, source_target_pairs={{0,504},{4,508},{8,0},{12,4},{16,8},{20,12},{24,16},{28,20},{32,24... | collective-permute-start | bytes 737288 | tf_op jit(solution)/shard_map/ppermute | solution.py:14
  116.6 33.7 %collective-permute-start.13 = (bf16[2,3,32,640]{3,2,1,0:T(8,128)(2,1)}, bf16[2,3,32,640]{3,2,1,0:T(8,128)(2,1)S(1)}, u32[]{:S(2)}, u32[]{:S(2)}) collective-permute-start(bf16[2,3,32,640]{3,2,1,0:T(8,128)(2,1)} %bitcast.38), channel_id=1, source_target_pairs={{0,500},{4,504},{8,508},{12,0},{16,4},{20,8},{24,12},{28,16},{32,2... | collective-permute-start | bytes 737288 | tf_op jit(solution)/shard_map/ppermute | solution.py:14
  120.4 31.9 %collective-permute-start.14 = (bf16[2,3,32,640]{3,2,1,0:T(8,128)(2,1)}, bf16[2,3,32,640]{3,2,1,0:T(8,128)(2,1)S(1)}, u32[]{:S(2)}, u32[]{:S(2)}) collective-permute-start(bf16[2,3,32,640]{3,2,1,0:T(8,128)(2,1)} %bitcast.39), channel_id=1, source_target_pairs={{0,496},{4,500},{8,504},{12,508},{16,0},{20,4},{24,8},{28,12},{32,... | collective-permute-start | bytes 737288 | tf_op jit(solution)/shard_map/ppermute | solution.py:14
  132.4 22.8 %collective-permute-start.15 = (bf16[2,3,32,640]{3,2,1,0:T(8,128)(2,1)}, bf16[2,3,32,640]{3,2,1,0:T(8,128)(2,1)S(1)}, u32[]{:S(2)}, u32[]{:S(2)}) collective-permute-start(bf16[2,3,32,640]{3,2,1,0:T(8,128)(2,1)} %bitcast.40), channel_id=1, source_target_pairs={{0,492},{4,496},{8,500},{12,504},{16,508},{20,0},{24,4},{28,8},{32... | collective-permute-start | bytes 737288 | tf_op jit(solution)/shard_map/ppermute | solution.py:14
  135.3 37.2 %collective-permute-start.16 = (bf16[2,3,32,640]{3,2,1,0:T(8,128)(2,1)S(1)}, bf16[2,3,32,640]{3,2,1,0:T(8,128)(2,1)S(1)}, u32[]{:S(2)}, u32[]{:S(2)}) collective-permute-start(bf16[2,3,32,640]{3,2,1,0:T(8,128)(2,1)S(1)} %bitcast.42), channel_id=1, source_target_pairs={{0,488},{4,492},{8,496},{12,500},{16,504},{20,508},{24,0},{28,4},{... | collective-permute-start | bytes 737288 | tf_op jit(solution)/shard_map/ppermute | solution.py:14
  142.9 37.6 %collective-permute-start.17 = (bf16[2,3,32,640]{3,2,1,0:T(8,128)(2,1)S(1)}, bf16[2,3,32,640]{3,2,1,0:T(8,128)(2,1)S(1)}, u32[]{:S(2)}, u32[]{:S(2)}) collective-permute-start(bf16[2,3,32,640]{3,2,1,0:T(8,128)(2,1)S(1)} %bitcast.43), channel_id=1, source_target_pairs={{0,484},{4,488},{8,492},{12,496},{16,500},{20,504},{24,508},{28,0}... | collective-permute-start | bytes 737288 | tf_op jit(solution)/shard_map/ppermute | solution.py:14
  150.3 30.3 %collective-permute-start.18 = (bf16[2,3,32,640]{3,2,1,0:T(8,128)(2,1)S(1)}, bf16[2,3,32,640]{3,2,1,0:T(8,128)(2,1)S(1)}, u32[]{:S(2)}, u32[]{:S(2)}) collective-permute-start(bf16[2,3,32,640]{3,2,1,0:T(8,128)(2,1)S(1)} %bitcast.44), channel_id=1, source_target_pairs={{0,480},{4,484},{8,488},{12,492},{16,496},{20,500},{24,504},{28,50... | collective-permute-start | bytes 737288 | tf_op jit(solution)/shard_map/ppermute | solution.py:14
  152.3 28.3 %collective-permute-start.19 = (bf16[2,3,32,640]{3,2,1,0:T(8,128)(2,1)S(1)}, bf16[2,3,32,640]{3,2,1,0:T(8,128)(2,1)S(1)}, u32[]{:S(2)}, u32[]{:S(2)}) collective-permute-start(bf16[2,3,32,640]{3,2,1,0:T(8,128)(2,1)S(1)} %bitcast.45), channel_id=1, source_target_pairs={{0,476},{4,480},{8,484},{12,488},{16,492},{20,496},{24,500},{28,50... | collective-permute-start | bytes 737288 | tf_op jit(solution)/shard_map/ppermute | solution.py:14
  155.2 58.0 %collective-permute-start.20 = (bf16[2,3,32,640]{3,2,1,0:T(8,128)(2,1)S(1)}, bf16[2,3,32,640]{3,2,1,0:T(8,128)(2,1)S(1)}, u32[]{:S(2)}, u32[]{:S(2)}) collective-permute-start(bf16[2,3,32,640]{3,2,1,0:T(8,128)(2,1)S(1)} %bitcast.46), channel_id=1, source_target_pairs={{0,472},{4,476},{8,480},{12,484},{16,488},{20,492},{24,496},{28,50... | collective-permute-start | bytes 737288 | tf_op jit(solution)/shard_map/ppermute | solution.py:14
  172.5 40.7 %collective-permute-start.21 = (bf16[2,3,32,640]{3,2,1,0:T(8,128)(2,1)S(1)}, bf16[2,3,32,640]{3,2,1,0:T(8,128)(2,1)S(1)}, u32[]{:S(2)}, u32[]{:S(2)}) collective-permute-start(bf16[2,3,32,640]{3,2,1,0:T(8,128)(2,1)S(1)} %bitcast.47), channel_id=1, source_target_pairs={{0,468},{4,472},{8,476},{12,480},{16,484},{20,488},{24,492},{28,49... | collective-permute-start | bytes 737288 | tf_op jit(solution)/shard_map/ppermute | solution.py:14
  (2 other events, 129.7 us)
Sparse Core Ops, SparseCore 0:
  9.4 605.4 all-gather.1
  621.0 112.2 reduce-scatter.1
where the time goes:
time: 741 us; the launch traced here: 740 us
  waiting for transfers between devices  582 us (79%)
  starting transfers between devices  130 us (18%)
  between operations  14 us (2%)
  matrix products  10.6 us (1%)
    all_gather x1, waiting for transfers between devices, on_device(): lax.all_gather(out_weight, 'frames', axis=1, tiled=True)  395 us
    ppermute x22, starting transfers between devices, from_behind(): lax.ppermute(x, axis, [(i, (i + by) % devices) for i in range(devices)])  130 us
    reduce_scatter x1, waiting for transfers between devices, on_device(): lax.psum_scatter(partial_rows.astype(jnp.bfloat16), 'heads', scatter_dime...  112 us
    ppermute x22, waiting for transfers between devices, from_behind(): lax.ppermute(x, axis, [(i, (i + by) % devices) for i in range(devices)])  74 us
  transfers between devices with their start and end apart: 24, of which 10 were waited for; matrix products, arithmetic and copies ran while one was open for 1% of the time, Pallas kernels for 0%

commit v1 on v0

--- a/solution.py
+++ b/solution.py
@@ -57,7 +57,15 @@
     attended = jnp.concatenate(results, axis=1)
     partial_rows = jnp.dot(
         attended,
-        lax.all_gather(out_weight, "frames", axis=1, tiled=True),
+        jnp.concatenate(
+            jax.lax.all_to_all(
+                jnp.stack([out_weight for _ in range(jax.lax.axis_size("frames"))], axis=0),
+                "frames",
+                0,
+                0,
+            ),
+            axis=1,
+        ),
         preferred_element_type=jnp.float32,
     )
     return lax.psum_scatter(

time: 741 us -> 473 us (0.64)
  waiting for transfers between devices: 582 us -> 288 us
  starting transfers between devices: 130 us -> 154 us
    all_gather x1 -> x0, waiting for transfers between devices: 395 us -> none  [on_device(): lax.all_gather(out_weight, 'frames', axis=1, tiled=True)]
    ppermute x22, waiting for transfers between devices: 74 us -> 226 us  [from_behind(): lax.ppermute(x, axis, [(i, (i + by) % devices) for i in range(devices)])]
    reduce_scatter x1, waiting for transfers between devices: 112 us -> 62.4 us  [on_device(): lax.psum_scatter(partial_rows.astype(jnp.bfloat16), 'heads', scatter_dime...]
    all_to_all x0 -> x1, starting transfers between devices: none -> 19.9 us  [on_device(): jax.lax.all_to_all(jnp.stack([out_weight for _ in range(jax.lax.axis_size...]
  transfers between devices with their start and end apart: 24 -> 24, of which waited for: 10 -> 13; matrix products, arithmetic and copies ran while one was open for 1% -> 1% of each run, Pallas kernels for 0% -> 0%
where the time goes in v1:
time: 473 us
  waiting for transfers between devices  288 us (61%)
  starting transfers between devices  154 us (33%)
  between operations  13.9 us (3%)
  matrix products  10.6 us (2%)
  local copies, waits for them, and re-layouts  5.23 us (1%)
    ppermute x22, waiting for transfers between devices, from_behind(): lax.ppermute(x, axis, [(i, (i + by) % devices) for i in range(devices)])  226 us
    ppermute x22, starting transfers between devices, from_behind(): lax.ppermute(x, axis, [(i, (i + by) % devices) for i in range(devices)])  134 us
    reduce_scatter x1, waiting for transfers between devices, on_device(): lax.psum_scatter(partial_rows.astype(jnp.bfloat16), 'heads', scatter_dime...  62.4 us
    all_to_all x1, starting transfers between devices, on_device(): jax.lax.all_to_all(jnp.stack([out_weight for _ in range(jax.lax.axis_size...  19.9 us
  transfers between devices with their start and end apart: 24, of which 13 were waited for; matrix products, arithmetic and copies ran while one was open for 1% of the time, Pallas kernels for 0%

profile of v1, /device:TPU:1, one launch (start us, length us, event | category | flops | bytes accessed | tf_op | source)
XLA Modules:
  0.0 472.5 jit_solution(2914670286374518467)
XLA Ops:
  10.6 19.9 %all-to-all-start = ((bf16[128,640,40]{1,2,0:T(8,128)(2,1)}), bf16[128,640,40]{1,2,0:T(8,128)(2,1)}, u32[]{:S(2)}, u32[]{:S(2)}) async-start(bf16[128,640,40]{1,2,0:T(8,128)(2,1)} %stack.2), calls=%async_computation | async-start | bytes 13107200 | tf_op jit(solution)/shard_map/all_to_all | solution.py:61
  30.5 6.3 %collective-permute-start = (bf16[2,3,32,640]{3,2,1,0:T(8,128)(2,1)S(1)}, bf16[2,3,32,640]{3,2,1,0:T(8,128)(2,1)S(1)}, u32[]{:S(2)}, u32[]{:S(2)}) collective-permute-start(bf16[2,3,32,640]{3,2,1,0:T(8,128)(2,1)S(1)} %bitcast.28), channel_id=1, source_target_pairs={{0,44},{4,48},{8,52},{12,56},{16,60},{20,64},{24,68},{28,72},{32,7... | collective-permute-start | bytes 737288 | tf_op jit(solution)/shard_map/ppermute | solution.py:14
  40.9 4.4 collective-permute-start.2
  45.2 5.8 %collective-permute-start.3 = (bf16[2,3,32,640]{3,2,1,0:T(8,128)(2,1)S(1)}, bf16[2,3,32,640]{3,2,1,0:T(8,128)(2,1)S(1)}, u32[]{:S(2)}, u32[]{:S(2)}) collective-permute-start(bf16[2,3,32,640]{3,2,1,0:T(8,128)(2,1)S(1)} %bitcast.31), channel_id=1, source_target_pairs={{0,32},{4,36},{8,40},{12,44},{16,48},{20,52},{24,56},{28,60},{32,6... | collective-permute-start | bytes 737288 | tf_op jit(solution)/shard_map/ppermute | solution.py:14
  51.1 4.0 collective-permute-start.4
  55.1 134.2 %collective-permute-done = bf16[2,3,32,640]{3,2,1,0:T(8,128)(2,1)S(1)} collective-permute-done((bf16[2,3,32,640]{3,2,1,0:T(8,128)(2,1)S(1)}, bf16[2,3,32,640]{3,2,1,0:T(8,128)(2,1)S(1)}, u32[]{:S(2)}, u32[]{:S(2)}) %collective-permute-start) | collective-permute-done | bytes 245792 | tf_op jit(solution)/shard_map/ppermute | solution.py:14
  191.3 36.0 %collective-permute-done.1 = bf16[2,3,32,640]{3,2,1,0:T(8,128)(2,1)S(1)} collective-permute-done((bf16[2,3,32,640]{3,2,1,0:T(8,128)(2,1)S(1)}, bf16[2,3,32,640]{3,2,1,0:T(8,128)(2,1)S(1)}, u32[]{:S(2)}, u32[]{:S(2)}) %collective-permute-start.1) | collective-permute-done | bytes 245792 | tf_op jit(solution)/shard_map/ppermute | solution.py:14
  229.3 8.1 %collective-permute-done.2 = bf16[2,3,32,640]{3,2,1,0:T(8,128)(2,1)S(1)} collective-permute-done((bf16[2,3,32,640]{3,2,1,0:T(8,128)(2,1)S(1)}, bf16[2,3,32,640]{3,2,1,0:T(8,128)(2,1)S(1)}, u32[]{:S(2)}, u32[]{:S(2)}) %collective-permute-start.2) | collective-permute-done | bytes 245792 | tf_op jit(solution)/shard_map/ppermute | solution.py:14
  237.4 7.7 %collective-permute-start.7 = (bf16[2,3,32,640]{3,2,1,0:T(8,128)(2,1)S(1)}, bf16[2,3,32,640]{3,2,1,0:T(8,128)(2,1)S(1)}, u32[]{:S(2)}, u32[]{:S(2)}) collective-permute-start(bf16[2,3,32,640]{3,2,1,0:T(8,128)(2,1)S(1)} %bitcast.35), channel_id=1, source_target_pairs={{0,16},{4,20},{8,24},{12,28},{16,32},{20,36},{24,40},{28,44},{32,4... | collective-permute-start | bytes 737288 | tf_op jit(solution)/shard_map/ppermute | solution.py:14
  250.2 7.1 %collective-permute-start.9 = (bf16[2,3,32,640]{3,2,1,0:T(8,128)(2,1)S(1)}, bf16[2,3,32,640]{3,2,1,0:T(8,128)(2,1)S(1)}, u32[]{:S(2)}, u32[]{:S(2)}) collective-permute-start(bf16[2,3,32,640]{3,2,1,0:T(8,128)(2,1)S(1)} %bitcast.37), channel_id=1, source_target_pairs={{0,8},{4,12},{8,16},{12,20},{16,24},{20,28},{24,32},{28,36},{32,40... | collective-permute-start | bytes 737288 | tf_op jit(solution)/shard_map/ppermute | solution.py:14
  260.6 4.7 collective-permute-done.6
  275.8 9.6 %collective-permute-start.13 = (bf16[2,3,32,640]{3,2,1,0:T(8,128)(2,1)S(1)}, bf16[2,3,32,640]{3,2,1,0:T(8,128)(2,1)S(1)}, u32[]{:S(2)}, u32[]{:S(2)}) collective-permute-start(bf16[2,3,32,640]{3,2,1,0:T(8,128)(2,1)S(1)} %bitcast.41), channel_id=1, source_target_pairs={{0,500},{4,504},{8,508},{12,0},{16,4},{20,8},{24,12},{28,16},{32,2... | collective-permute-start | bytes 737288 | tf_op jit(solution)/shard_map/ppermute | solution.py:14
  285.5 5.6 %collective-permute-start.14 = (bf16[2,3,32,640]{3,2,1,0:T(8,128)(2,1)S(1)}, bf16[2,3,32,640]{3,2,1,0:T(8,128)(2,1)S(1)}, u32[]{:S(2)}, u32[]{:S(2)}) collective-permute-start(bf16[2,3,32,640]{3,2,1,0:T(8,128)(2,1)S(1)} %bitcast.42), channel_id=1, source_target_pairs={{0,496},{4,500},{8,504},{12,508},{16,0},{20,4},{24,8},{28,12},{32,... | collective-permute-start | bytes 737288 | tf_op jit(solution)/shard_map/ppermute | solution.py:14
  293.3 10.7 %collective-permute-start.15 = (bf16[2,3,32,640]{3,2,1,0:T(8,128)(2,1)S(1)}, bf16[2,3,32,640]{3,2,1,0:T(8,128)(2,1)S(1)}, u32[]{:S(2)}, u32[]{:S(2)}) collective-permute-start(bf16[2,3,32,640]{3,2,1,0:T(8,128)(2,1)S(1)} %bitcast.43), channel_id=1, source_target_pairs={{0,492},{4,496},{8,500},{12,504},{16,508},{20,0},{24,4},{28,8},{32... | collective-permute-start | bytes 737288 | tf_op jit(solution)/shard_map/ppermute | solution.py:14
  304.1 4.9 %collective-permute-start.16 = (bf16[2,3,32,640]{3,2,1,0:T(8,128)(2,1)S(1)}, bf16[2,3,32,640]{3,2,1,0:T(8,128)(2,1)S(1)}, u32[]{:S(2)}, u32[]{:S(2)}) collective-permute-start(bf16[2,3,32,640]{3,2,1,0:T(8,128)(2,1)S(1)} %bitcast.45), channel_id=1, source_target_pairs={{0,488},{4,492},{8,496},{12,500},{16,504},{20,508},{24,0},{28,4},{... | collective-permute-start | bytes 737288 | tf_op jit(solution)/shard_map/ppermute | solution.py:14
  309.1 11.4 %collective-permute-start.17 = (bf16[2,3,32,640]{3,2,1,0:T(8,128)(2,1)S(1)}, bf16[2,3,32,640]{3,2,1,0:T(8,128)(2,1)S(1)}, u32[]{:S(2)}, u32[]{:S(2)}) collective-permute-start(bf16[2,3,32,640]{3,2,1,0:T(8,128)(2,1)S(1)} %bitcast.46), channel_id=1, source_target_pairs={{0,484},{4,488},{8,492},{12,496},{16,500},{20,504},{24,508},{28,0}... | collective-permute-start | bytes 737288 | tf_op jit(solution)/shard_map/ppermute | solution.py:14
  320.6 5.1 %collective-permute-start.18 = (bf16[2,3,32,640]{3,2,1,0:T(8,128)(2,1)S(1)}, bf16[2,3,32,640]{3,2,1,0:T(8,128)(2,1)S(1)}, u32[]{:S(2)}, u32[]{:S(2)}) collective-permute-start(bf16[2,3,32,640]{3,2,1,0:T(8,128)(2,1)S(1)} %bitcast.47), channel_id=1, source_target_pairs={{0,480},{4,484},{8,488},{12,492},{16,496},{20,500},{24,504},{28,50... | collective-permute-start | bytes 737288 | tf_op jit(solution)/shard_map/ppermute | solution.py:14
  325.8 14.9 %collective-permute-start.19 = (bf16[2,3,32,640]{3,2,1,0:T(8,128)(2,1)S(1)}, bf16[2,3,32,640]{3,2,1,0:T(8,128)(2,1)S(1)}, u32[]{:S(2)}, u32[]{:S(2)}) collective-permute-start(bf16[2,3,32,640]{3,2,1,0:T(8,128)(2,1)S(1)} %bitcast.48), channel_id=1, source_target_pairs={{0,476},{4,480},{8,484},{12,488},{16,492},{20,496},{24,500},{28,50... | collective-permute-start | bytes 737288 | tf_op jit(solution)/shard_map/ppermute | solution.py:14
  343.8 16.1 %collective-permute-start.21 = (bf16[2,3,32,640]{3,2,1,0:T(8,128)(2,1)S(1)}, bf16[2,3,32,640]{3,2,1,0:T(8,128)(2,1)S(1)}, u32[]{:S(2)}, u32[]{:S(2)}) collective-permute-start(bf16[2,3,32,640]{3,2,1,0:T(8,128)(2,1)S(1)} %bitcast.50), channel_id=1, source_target_pairs={{0,468},{4,472},{8,476},{12,480},{16,484},{20,488},{24,492},{28,49... | collective-permute-start | bytes 737288 | tf_op jit(solution)/shard_map/ppermute | solution.py:14
  360.0 4.8 %collective-permute-done.19 = bf16[2,3,32,640]{3,2,1,0:T(8,128)(2,1)S(1)} collective-permute-done((bf16[2,3,32,640]{3,2,1,0:T(8,128)(2,1)S(1)}, bf16[2,3,32,640]{3,2,1,0:T(8,128)(2,1)S(1)}, u32[]{:S(2)}, u32[]{:S(2)}) %collective-permute-start.19) | collective-permute-done | bytes 245792 | tf_op jit(solution)/shard_map/ppermute | solution.py:14
  364.8 16.5 %collective-permute-done.20 = bf16[2,3,32,640]{3,2,1,0:T(8,128)(2,1)S(1)} collective-permute-done((bf16[2,3,32,640]{3,2,1,0:T(8,128)(2,1)S(1)}, bf16[2,3,32,640]{3,2,1,0:T(8,128)(2,1)S(1)}, u32[]{:S(2)}, u32[]{:S(2)}) %collective-permute-start.20) | collective-permute-done | bytes 245792 | tf_op jit(solution)/shard_map/ppermute | solution.py:14
  381.3 10.0 %collective-permute-done.21 = bf16[2,3,32,640]{3,2,1,0:T(8,128)(2,1)S(1)} collective-permute-done((bf16[2,3,32,640]{3,2,1,0:T(8,128)(2,1)S(1)}, bf16[2,3,32,640]{3,2,1,0:T(8,128)(2,1)S(1)}, u32[]{:S(2)}, u32[]{:S(2)}) %collective-permute-start.21) | collective-permute-done | bytes 245792 | tf_op jit(solution)/shard_map/ppermute | solution.py:14
  397.3 5.9 %convolution_convert_fusion = bf16[96,5120]{1,0:T(8,128)(2,1)} fusion(bf16[96,640]{1,0:T(8,128)(2,1)S(1)} %fusion.5, bf16[640,5120]{0,1:T(8,128)(2,1)} %bitcast.9), kind=kOutput, calls=%fused_computation | convolution fusion | flops 629637120 | bytes 7659520 | tf_op jit(solution)/shard_map/dot_general | solution.py:58
  403.3 62.4 %reduce-scatter.2.cloned.1.call-done = bf16[96,1280]{1,0:T(8,128)(2,1)} async-done(((bf16[96,5120]{1,0:T(8,128)(2,1)}), bf16[96,1280]{1,0:T(8,128)(2,1)}) %reduce-scatter.2.cloned.1.call-update) | async-done | bytes 245776 | tf_op jit(solution)/shard_map/reduce_scatter | solution.py:71
  (68 shorter events, 42.3 us)
Async XLA Ops:
  10.6 386.8 %all-to-all-start = ((bf16[128,640,40]{1,2,0:T(8,128)(2,1)}), bf16[128,640,40]{1,2,0:T(8,128)(2,1)}, u32[]{:S(2)}, u32[]{:S(2)}) async-start(bf16[128,640,40]{1,2,0:T(8,128)(2,1)} %stack.2), calls=%async_computation | async-start | bytes 13107200 | tf_op jit(solution)/shard_map/all_to_all | solution.py:61
  30.4 435.3 %reduce-scatter.2.cloned.1.call-start = ((), (), s32[]{:S(2)}) async-start(), calls=%async_computation.2 | async-start | bytes 1228800 | tf_op jit(solution)/shard_map/reduce_scatter | solution.py:71
  30.5 158.9 %collective-permute-start = (bf16[2,3,32,640]{3,2,1,0:T(8,128)(2,1)S(1)}, bf16[2,3,32,640]{3,2,1,0:T(8,128)(2,1)S(1)}, u32[]{:S(2)}, u32[]{:S(2)}) collective-permute-start(bf16[2,3,32,640]{3,2,1,0:T(8,128)(2,1)S(1)} %bitcast.28), channel_id=1, source_target_pairs={{0,44},{4,48},{8,52},{12,56},{16,60},{20,64},{24,68},{28,72},{32,7... | collective-permute-start | bytes 737288 | tf_op jit(solution)/shard_map/ppermute | solution.py:14
  36.8 190.5 %collective-permute-start.1 = (bf16[2,3,32,640]{3,2,1,0:T(8,128)(2,1)S(1)}, bf16[2,3,32,640]{3,2,1,0:T(8,128)(2,1)S(1)}, u32[]{:S(2)}, u32[]{:S(2)}) collective-permute-start(bf16[2,3,32,640]{3,2,1,0:T(8,128)(2,1)S(1)} %bitcast.29), channel_id=1, source_target_pairs={{0,40},{4,44},{8,48},{12,52},{16,56},{20,60},{24,64},{28,68},{32,7... | collective-permute-start | bytes 737288 | tf_op jit(solution)/shard_map/ppermute | solution.py:14
  40.9 196.6 %collective-permute-start.2 = (bf16[2,3,32,640]{3,2,1,0:T(8,128)(2,1)S(1)}, bf16[2,3,32,640]{3,2,1,0:T(8,128)(2,1)S(1)}, u32[]{:S(2)}, u32[]{:S(2)}) collective-permute-start(bf16[2,3,32,640]{3,2,1,0:T(8,128)(2,1)S(1)} %bitcast.30), channel_id=1, source_target_pairs={{0,36},{4,40},{8,44},{12,48},{16,52},{20,56},{24,60},{28,64},{32,6... | collective-permute-start | bytes 737288 | tf_op jit(solution)/shard_map/ppermute | solution.py:14
  45.2 199.9 %collective-permute-start.3 = (bf16[2,3,32,640]{3,2,1,0:T(8,128)(2,1)S(1)}, bf16[2,3,32,640]{3,2,1,0:T(8,128)(2,1)S(1)}, u32[]{:S(2)}, u32[]{:S(2)}) collective-permute-start(bf16[2,3,32,640]{3,2,1,0:T(8,128)(2,1)S(1)} %bitcast.31), channel_id=1, source_target_pairs={{0,32},{4,36},{8,40},{12,44},{16,48},{20,52},{24,56},{28,60},{32,6... | collective-permute-start | bytes 737288 | tf_op jit(solution)/shard_map/ppermute | solution.py:14
  51.1 199.2 %collective-permute-start.4 = (bf16[2,3,32,640]{3,2,1,0:T(8,128)(2,1)S(1)}, bf16[2,3,32,640]{3,2,1,0:T(8,128)(2,1)S(1)}, u32[]{:S(2)}, u32[]{:S(2)}) collective-permute-start(bf16[2,3,32,640]{3,2,1,0:T(8,128)(2,1)S(1)} %bitcast.32), channel_id=1, source_target_pairs={{0,28},{4,32},{8,36},{12,40},{16,44},{20,48},{24,52},{28,56},{32,6... | collective-permute-start | bytes 737288 | tf_op jit(solution)/shard_map/ppermute | solution.py:14
  189.4 69.2 %collective-permute-start.5 = (bf16[2,3,32,640]{3,2,1,0:T(8,128)(2,1)S(1)}, bf16[2,3,32,640]{3,2,1,0:T(8,128)(2,1)S(1)}, u32[]{:S(2)}, u32[]{:S(2)}) collective-permute-start(bf16[2,3,32,640]{3,2,1,0:T(8,128)(2,1)S(1)} %bitcast.33), channel_id=1, source_target_pairs={{0,24},{4,28},{8,32},{12,36},{16,40},{20,44},{24,48},{28,52},{32,5... | collective-permute-start | bytes 737288 | tf_op jit(solution)/shard_map/ppermute | solution.py:14
  227.3 38.0 %collective-permute-start.6 = (bf16[2,3,32,640]{3,2,1,0:T(8,128)(2,1)S(1)}, bf16[2,3,32,640]{3,2,1,0:T(8,128)(2,1)S(1)}, u32[]{:S(2)}, u32[]{:S(2)}) collective-permute-start(bf16[2,3,32,640]{3,2,1,0:T(8,128)(2,1)S(1)} %bitcast.34), channel_id=1, source_target_pairs={{0,20},{4,24},{8,28},{12,32},{16,36},{20,40},{24,44},{28,48},{32,5... | collective-permute-start | bytes 737288 | tf_op jit(solution)/shard_map/ppermute | solution.py:14
  237.4 33.2 %collective-permute-start.7 = (bf16[2,3,32,640]{3,2,1,0:T(8,128)(2,1)S(1)}, bf16[2,3,32,640]{3,2,1,0:T(8,128)(2,1)S(1)}, u32[]{:S(2)}, u32[]{:S(2)}) collective-permute-start(bf16[2,3,32,640]{3,2,1,0:T(8,128)(2,1)S(1)} %bitcast.35), channel_id=1, source_target_pairs={{0,16},{4,20},{8,24},{12,28},{16,32},{20,36},{24,40},{28,44},{32,4... | collective-permute-start | bytes 737288 | tf_op jit(solution)/shard_map/ppermute | solution.py:14
  245.1 30.7 %collective-permute-start.8 = (bf16[2,3,32,640]{3,2,1,0:T(8,128)(2,1)S(1)}, bf16[2,3,32,640]{3,2,1,0:T(8,128)(2,1)S(1)}, u32[]{:S(2)}, u32[]{:S(2)}) collective-permute-start(bf16[2,3,32,640]{3,2,1,0:T(8,128)(2,1)S(1)} %bitcast.36), channel_id=1, source_target_pairs={{0,12},{4,16},{8,20},{12,24},{16,28},{20,32},{24,36},{28,40},{32,4... | collective-permute-start | bytes 737288 | tf_op jit(solution)/shard_map/ppermute | solution.py:14
  250.2 35.3 %collective-permute-start.9 = (bf16[2,3,32,640]{3,2,1,0:T(8,128)(2,1)S(1)}, bf16[2,3,32,640]{3,2,1,0:T(8,128)(2,1)S(1)}, u32[]{:S(2)}, u32[]{:S(2)}) collective-permute-start(bf16[2,3,32,640]{3,2,1,0:T(8,128)(2,1)S(1)} %bitcast.37), channel_id=1, source_target_pairs={{0,8},{4,12},{8,16},{12,20},{16,24},{20,28},{24,32},{28,36},{32,40... | collective-permute-start | bytes 737288 | tf_op jit(solution)/shard_map/ppermute | solution.py:14
  258.6 34.7 %collective-permute-start.10 = (bf16[2,3,32,640]{3,2,1,0:T(8,128)(2,1)S(1)}, bf16[2,3,32,640]{3,2,1,0:T(8,128)(2,1)S(1)}, u32[]{:S(2)}, u32[]{:S(2)}) collective-permute-start(bf16[2,3,32,640]{3,2,1,0:T(8,128)(2,1)S(1)} %bitcast.38), channel_id=1, source_target_pairs={{0,4},{4,8},{8,12},{12,16},{16,20},{20,24},{24,28},{28,32},{32,36}... | collective-permute-start | bytes 737288 | tf_op jit(solution)/shard_map/ppermute | solution.py:14
  265.3 38.8 %collective-permute-start.11 = (bf16[2,3,32,640]{3,2,1,0:T(8,128)(2,1)S(1)}, bf16[2,3,32,640]{3,2,1,0:T(8,128)(2,1)S(1)}, u32[]{:S(2)}, u32[]{:S(2)}) collective-permute-start(bf16[2,3,32,640]{3,2,1,0:T(8,128)(2,1)S(1)} %bitcast.39), channel_id=1, source_target_pairs={{0,508},{4,0},{8,4},{12,8},{16,12},{20,16},{24,20},{28,24},{32,28}... | collective-permute-start | bytes 737288 | tf_op jit(solution)/shard_map/ppermute | solution.py:14
  270.6 38.5 %collective-permute-start.12 = (bf16[2,3,32,640]{3,2,1,0:T(8,128)(2,1)S(1)}, bf16[2,3,32,640]{3,2,1,0:T(8,128)(2,1)S(1)}, u32[]{:S(2)}, u32[]{:S(2)}) collective-permute-start(bf16[2,3,32,640]{3,2,1,0:T(8,128)(2,1)S(1)} %bitcast.40), channel_id=1, source_target_pairs={{0,504},{4,508},{8,0},{12,4},{16,8},{20,12},{24,16},{28,20},{32,24... | collective-permute-start | bytes 737288 | tf_op jit(solution)/shard_map/ppermute | solution.py:14
  275.8 44.7 %collective-permute-start.13 = (bf16[2,3,32,640]{3,2,1,0:T(8,128)(2,1)S(1)}, bf16[2,3,32,640]{3,2,1,0:T(8,128)(2,1)S(1)}, u32[]{:S(2)}, u32[]{:S(2)}) collective-permute-start(bf16[2,3,32,640]{3,2,1,0:T(8,128)(2,1)S(1)} %bitcast.41), channel_id=1, source_target_pairs={{0,500},{4,504},{8,508},{12,0},{16,4},{20,8},{24,12},{28,16},{32,2... | collective-permute-start | bytes 737288 | tf_op jit(solution)/shard_map/ppermute | solution.py:14
  285.5 40.2 %collective-permute-start.14 = (bf16[2,3,32,640]{3,2,1,0:T(8,128)(2,1)S(1)}, bf16[2,3,32,640]{3,2,1,0:T(8,128)(2,1)S(1)}, u32[]{:S(2)}, u32[]{:S(2)}) collective-permute-start(bf16[2,3,32,640]{3,2,1,0:T(8,128)(2,1)S(1)} %bitcast.42), channel_id=1, source_target_pairs={{0,496},{4,500},{8,504},{12,508},{16,0},{20,4},{24,8},{28,12},{32,... | collective-permute-start | bytes 737288 | tf_op jit(solution)/shard_map/ppermute | solution.py:14
  293.3 47.4 %collective-permute-start.15 = (bf16[2,3,32,640]{3,2,1,0:T(8,128)(2,1)S(1)}, bf16[2,3,32,640]{3,2,1,0:T(8,128)(2,1)S(1)}, u32[]{:S(2)}, u32[]{:S(2)}) collective-permute-start(bf16[2,3,32,640]{3,2,1,0:T(8,128)(2,1)S(1)} %bitcast.43), channel_id=1, source_target_pairs={{0,492},{4,496},{8,500},{12,504},{16,508},{20,0},{24,4},{28,8},{32... | collective-permute-start | bytes 737288 | tf_op jit(solution)/shard_map/ppermute | solution.py:14
  304.1 39.6 %collective-permute-start.16 = (bf16[2,3,32,640]{3,2,1,0:T(8,128)(2,1)S(1)}, bf16[2,3,32,640]{3,2,1,0:T(8,128)(2,1)S(1)}, u32[]{:S(2)}, u32[]{:S(2)}) collective-permute-start(bf16[2,3,32,640]{3,2,1,0:T(8,128)(2,1)S(1)} %bitcast.45), channel_id=1, source_target_pairs={{0,488},{4,492},{8,496},{12,500},{16,504},{20,508},{24,0},{28,4},{... | collective-permute-start | bytes 737288 | tf_op jit(solution)/shard_map/ppermute | solution.py:14
  309.1 50.8 %collective-permute-start.17 = (bf16[2,3,32,640]{3,2,1,0:T(8,128)(2,1)S(1)}, bf16[2,3,32,640]{3,2,1,0:T(8,128)(2,1)S(1)}, u32[]{:S(2)}, u32[]{:S(2)}) collective-permute-start(bf16[2,3,32,640]{3,2,1,0:T(8,128)(2,1)S(1)} %bitcast.46), channel_id=1, source_target_pairs={{0,484},{4,488},{8,492},{12,496},{16,500},{20,504},{24,508},{28,0}... | collective-permute-start | bytes 737288 | tf_op jit(solution)/shard_map/ppermute | solution.py:14
  320.6 39.4 %collective-permute-start.18 = (bf16[2,3,32,640]{3,2,1,0:T(8,128)(2,1)S(1)}, bf16[2,3,32,640]{3,2,1,0:T(8,128)(2,1)S(1)}, u32[]{:S(2)}, u32[]{:S(2)}) collective-permute-start(bf16[2,3,32,640]{3,2,1,0:T(8,128)(2,1)S(1)} %bitcast.47), channel_id=1, source_target_pairs={{0,480},{4,484},{8,488},{12,492},{16,496},{20,500},{24,504},{28,50... | collective-permute-start | bytes 737288 | tf_op jit(solution)/shard_map/ppermute | solution.py:14
  325.8 39.0 %collective-permute-start.19 = (bf16[2,3,32,640]{3,2,1,0:T(8,128)(2,1)S(1)}, bf16[2,3,32,640]{3,2,1,0:T(8,128)(2,1)S(1)}, u32[]{:S(2)}, u32[]{:S(2)}) collective-permute-start(bf16[2,3,32,640]{3,2,1,0:T(8,128)(2,1)S(1)} %bitcast.48), channel_id=1, source_target_pairs={{0,476},{4,480},{8,484},{12,488},{16,492},{20,496},{24,500},{28,50... | collective-permute-start | bytes 737288 | tf_op jit(solution)/shard_map/ppermute | solution.py:14
  340.7 40.6 %collective-permute-start.20 = (bf16[2,3,32,640]{3,2,1,0:T(8,128)(2,1)S(1)}, bf16[2,3,32,640]{3,2,1,0:T(8,128)(2,1)S(1)}, u32[]{:S(2)}, u32[]{:S(2)}) collective-permute-start(bf16[2,3,32,640]{3,2,1,0:T(8,128)(2,1)S(1)} %bitcast.49), channel_id=1, source_target_pairs={{0,472},{4,476},{8,480},{12,484},{16,488},{20,492},{24,496},{28,50... | collective-permute-start | bytes 737288 | tf_op jit(solution)/shard_map/ppermute | solution.py:14
  343.8 47.6 %collective-permute-start.21 = (bf16[2,3,32,640]{3,2,1,0:T(8,128)(2,1)S(1)}, bf16[2,3,32,640]{3,2,1,0:T(8,128)(2,1)S(1)}, u32[]{:S(2)}, u32[]{:S(2)}) collective-permute-start(bf16[2,3,32,640]{3,2,1,0:T(8,128)(2,1)S(1)} %bitcast.50), channel_id=1, source_target_pairs={{0,468},{4,472},{8,476},{12,480},{16,484},{20,488},{24,492},{28,49... | collective-permute-start | bytes 737288 | tf_op jit(solution)/shard_map/ppermute | solution.py:14
  (2 other events, 30.5 us)
Sparse Core Ops, SparseCore 0:
  403.4 62.2 reduce-scatter.1
